TPU v7x, 32 devices: a whole 2x2x4 slice. The times are simulated.
32 devices in a mesh: depth: 4 (over y, x), plane: 8 (over z, core).
Axes of the slice: x: 2, y: 2, z: 4, core: 2. Of those that a mesh axis runs over, the one named last changes fastest.
Arguments:
- volume: bfloat16 [16, 32, 128], P('depth', 'plane'), may hold values from -6 to 6
- cotangent: float32 [16, 32, 128], P('depth', 'plane'), may hold values from -6 to 6
- kernel_in: bfloat16 [27, 32], replicated, may hold values from -1.25 to 1.25
- kernel_mid: bfloat16 [27, 32, 32], replicated, may hold values from -0.21875 to 0.21875
- kernel_out: bfloat16 [27, 32], replicated, may hold values from -0.21875 to 0.21875
- measured: float32 [16, 32, 1024], P('depth'), may hold values from -24 to 24
- angle_ids: int32 [8], replicated, may hold values from 0 to 31, as said below
- ray_bins: int32 [8, 32, 128], P(None, 'plane'), may hold values from 0 to 1023, as said below
Outputs:
- grad_volume: float32 [16, 32, 128], P('depth', 'plane')
- grad_kernel_in: float32 [27, 32], replicated
- grad_kernel_mid: float32 [27, 32, 32], replicated
- grad_kernel_out: float32 [27, 32], replicated
Inputs may be any that keep to these rules, and one draw needn't show every extreme that they name: `angle_ids`: each entry names a measured view; the entries are distinct. `ray_bins`: for each view a, the bins follow parallel-beam geometry: a cell's bin is the detector position of its centre projected along the direction of view angle_ids[a], clipped at the detector's ends.
All inputs are finite; a program needn't handle non-finite values.
Results may differ from a plain program's by a relative error of at most 0.0051.
Values may be sent and summed in bfloat16 or wider, within the bound.
A program may use at most 64 MiB of HBM per device.

v0:
```python
import functools

import numpy as np
import jax
import jax.numpy as jnp
from jax import lax
from jax.experimental import pallas as pl
from jax.experimental.pallas import tpu as pltpu
from jax.sharding import PartitionSpec as P

MESH = pl.DeviceIdType.MESH
BF = jnp.bfloat16
F32 = jnp.float32
DELTA = 6.0
VMEM_LIMIT = 56 * 1024 * 1024
NT = (((1,), (1,)), ((), ()))


def mm(a, b):
    return jnp.dot(a, b, preferred_element_type=F32)


def mm_nt(a, b):
    return lax.dot_general(a, b, NT, preferred_element_type=F32)


def shift(x, j):
    if j == 1:
        return x
    width = x.shape[-1]
    lane = lax.broadcasted_iota(jnp.int32, x.shape, x.ndim - 1)
    if j == 0:
        return jnp.where(lane == 0, 0.0, pltpu.roll(x, 1, x.ndim - 1))
    return jnp.where(lane == width - 1, 0.0, pltpu.roll(x, width - 1, x.ndim - 1))


def sig(v):
    return 1.0 / (1.0 + jnp.exp(-v))


def halo_targets(depth, plane):
    d, p = lax.axis_index("depth"), lax.axis_index("plane")
    out = []
    for dz in (-1, 0, 1):
        for dy in (-1, 0, 1):
            if dz == 0 and dy == 0:
                continue
            there = (d + dz >= 0) & (d + dz < depth) & (p + dy >= 0) & (p + dy < plane)
            out.append((dz, dy, there, (d + dz, p + dy)))
    return out


def halo_copy(dz, dy, who, mine, slots, send, recv):
    slot = (1 - dz) * 3 + (1 - dy)
    return pltpu.make_async_remote_copy(
        src_ref=mine, dst_ref=slots.at[slot], send_sem=send.at[slot], recv_sem=recv.at[slot],
        device_id=who, device_id_type=MESH)


def halo_start(targets, mine, slots, send, recv):
    for dz, dy, there, who in targets:
        @pl.when(there)
        def _(dz=dz, dy=dy, who=who):
            halo_copy(dz, dy, who, mine, slots, send, recv).start()


def halo_wait(targets, mine, slots, send, recv):
    for dz, dy, there, who in targets:
        @pl.when(there)
        def _(dz=dz, dy=dy, who=who):
            halo_copy(dz, dy, who, mine, slots, send, recv).wait_send()
            halo_copy(-dz, -dy, who, mine, slots, send, recv).wait_recv()


def halo_kernel(depth, plane, block, out, slots, send, recv):
    targets = halo_targets(depth, plane)
    slots[...] = jnp.zeros_like(slots)
    bar = pltpu.get_barrier_semaphore()
    count = jnp.int32(0)
    for _, _, there, who in targets:
        @pl.when(there)
        def _(who=who):
            pl.semaphore_signal(bar, inc=1, device_id=who, device_id_type=MESH)
        count = count + there.astype(jnp.int32)
    pl.semaphore_wait(bar, count)
    halo_start(targets, block, slots, send, recv)
    halo_wait(targets, block, slots, send, recv)
    out[...] = slots[...]
    out[4] = block[...]


def fill_shifts(sel, slots, dst):
    flat = slots[...].reshape(9 * 16, 128)
    wide = mm(sel[...], flat)
    for z in range(12):
        rows = wide[z * 16:(z + 1) * 16]
        for j in range(3):
            dst[z * 48 + j * 16:z * 48 + (j + 1) * 16, :] = shift(rows, j).astype(BF)
    return wide


def keep_rows(shape, z, margin, depth, plane):
    d, p = lax.axis_index("depth"), lax.axis_index("plane")
    gz = d * 4 + z - margin
    row = lax.broadcasted_iota(jnp.int32, shape, 0)
    low = (margin - p * 4) * 32
    high = (plane * 4 + margin - p * 4) * 32
    high = jnp.where((gz >= 0) & (gz < depth * 4), high, -1)
    return (row >= low) & (row < high)


def build_onehot(bins, a, c, size):
    parts = []
    for y in range(4):
        row = bins[pl.ds(a * 4 + y, 1), :]
        at = lax.broadcasted_iota(jnp.int32, (size, 128), 0) + c * size
        parts.append(jnp.where(at == row, 1.0, 0.0).astype(BF))
    return jnp.concatenate(parts, axis=1)


def forward_kernel(depth, plane, lanes, slots, sel, t1, w2, t3, selp, cot, bins,
                   s_out, r_out, slope1, slope2, a2, proj):
    wide = fill_shifts(sel, slots, s_out)
    for z in range(10):
        pre = mm(t1[...], s_out[z * 48:z * 48 + 144, :])
        sg = sig(pre)
        keep = keep_rows(pre.shape, z, 3, depth, plane)
        act = jnp.where(keep, pre * sg, 0.0)
        for j in range(3):
            moved = shift(act, j).astype(BF)
            for y in range(10):
                r_out[z, y * 96 + j * 32:y * 96 + j * 32 + 32, :] = moved[y * 32:y * 32 + 32]
        if 2 <= z < 8:
            slope = jnp.where(keep, sg * (1.0 + pre * (1.0 - sg)), 0.0)
            slope1[z - 2] = slope[64:256]
    for y in range(0, 8, 2):
        res = []
        for z in range(10):
            rhs = jnp.concatenate(
                [r_out[z, y * 96:y * 96 + 288, :], r_out[z, y * 96 + 96:y * 96 + 384, :]], axis=1)
            res.append(mm(w2[...], rhs))
        for z in range(8):
            pre2 = res[z][0:32] + res[z + 1][32:64] + res[z + 2][64:96]
            for q in range(2):
                yy = y + q
                pre = pre2[:, q * 128:q * 128 + 128]
                sg = sig(pre)
                keep = keep_rows((256, 128), z, 2, depth, plane)[yy * 32:yy * 32 + 32]
                slope2[z, yy * 32:yy * 32 + 32, :] = jnp.where(
                    keep, sg * (1.0 + pre * (1.0 - sg)), 0.0)
                if 1 <= z < 7 and 1 <= yy < 7:
                    a2[z - 1, (yy - 1) * 32:yy * 32, :] = jnp.where(keep, pre * sg, 0.0).astype(BF)
    den = []
    res = [mm(t3[...], a2[z]) for z in range(6)]
    for z in range(4):
        total = wide[(z + 4) * 16:(z + 4) * 16 + 8]
        for j in range(3):
            part = res[z][j * 24:j * 24 + 8] + res[z + 1][j * 24 + 8:j * 24 + 16] \
                + res[z + 2][j * 24 + 16:j * 24 + 24]
            total = total - shift(part, j)
        den.append(total)
    both = jnp.concatenate(den + [cot[...]], axis=0)
    high = both.astype(BF)
    rest = (both - high.astype(F32)).astype(BF)
    stacked = mm(selp[...], jnp.concatenate([high, rest], axis=0)).astype(BF)
    lhs = jnp.concatenate([stacked[y * 16:y * 16 + 16] for y in range(4)], axis=1)
    per = 512 // lanes

    def view(a, carry):
        halves = []
        for half in range(2):
            row = []
            for c in range(2):
                got = mm_nt(lhs, build_onehot(bins, a, half * 2 + c, 256))
                row.append(got[0:8] + got[8:16])
            halves.append(jnp.concatenate(row, axis=1))
        full = jnp.concatenate(halves, axis=0)
        for q in range(per):
            proj[a * per + q] = full[:, q * lanes:(q + 1) * lanes]
        return carry

    lax.fori_loop(0, 8, view, 0)


def rays_kernel(depth, plane, lanes, proj, chosen, bins, cot, sely, gd_out, out,
                onehot, got, mine, ag, block, slots, send1, recv1, send2, recv2, send3, recv3):
    d, p = lax.axis_index("depth"), lax.axis_index("plane")
    targets = halo_targets(depth, plane)
    slots[...] = jnp.zeros_like(slots)
    bar = pltpu.get_barrier_semaphore()
    count = jnp.int32(plane - 1)
    for i in range(1, plane):
        pl.semaphore_signal(bar, inc=1, device_id=(d, lax.rem(p + i, plane)), device_id_type=MESH)
    for dz, _, there, who in targets:
        if dz != 0:
            @pl.when(there)
            def _(who=who):
                pl.semaphore_signal(bar, inc=1, device_id=who, device_id_type=MESH)
            count = count + there.astype(jnp.int32)
    pl.semaphore_wait(bar, count)

    def first(i):
        to = lax.rem(p + i, plane)
        return pltpu.make_async_remote_copy(
            src_ref=proj.at[to], dst_ref=got.at[i], send_sem=send1.at[i], recv_sem=recv1.at[i],
            device_id=(d, to), device_id_type=MESH)

    def second(i):
        to = lax.rem(p + i, plane)
        return pltpu.make_async_remote_copy(
            src_ref=mine, dst_ref=ag.at[p], send_sem=send2.at[i], recv_sem=recv2.at[i],
            device_id=(d, to), device_id_type=MESH)

    for i in range(1, plane):
        first(i).start()

    def fill(k, carry):
        a = k // 4
        c = lax.rem(k, 4)
        onehot[pl.ds(pl.multiple_of(k * 256, 256), 256), :] = build_onehot(bins, a, c, 256)
        return carry

    lax.fori_loop(0, 32, fill, 0)
    total = proj[p]
    for i in range(1, plane):
        first(i).wait_recv()
        total = total + got[i]
    ratio = (total - chosen[p]) / DELTA
    inner = 1.0 + ratio * ratio
    weighted = pltpu.roll(total, 12, 0) / (inner * jnp.sqrt(inner))
    lead = weighted.astype(BF).astype(F32)
    row = lax.rem(lax.broadcasted_iota(jnp.int32, weighted.shape, 0), 8)
    mine[...] = jnp.where(row < 4, lead, pltpu.roll(weighted - lead, 4, 0)).astype(BF)
    for i in range(1, plane):
        second(i).start()
    for i in range(1, plane):
        second(i).wait_recv()
        first(i).wait_send()
    for i in range(1, plane):
        second(i).wait_send()
    ag[p] = mine[...]
    per = 512 // lanes
    low = jnp.zeros((16, 512), F32)
    up = jnp.zeros((16, 512), F32)
    for a in range(8):
        lhs = jnp.concatenate([ag[a * per + q] for q in range(per)], axis=1)
        low = low + mm(lhs, onehot[a * 1024:a * 1024 + 512, :])
        up = up + mm(lhs, onehot[a * 1024 + 512:a * 1024 + 1024, :])
    up = pltpu.roll(up, 8, 0)
    back = low + up
    back = back + pltpu.roll(back, 12, 0)
    row = lax.broadcasted_iota(jnp.int32, (16, 512), 0)
    gd = jnp.where(row < 4, cot[...] - back * (0.25 / 8), 0.0)
    gd_out[...] = gd
    neg = (-gd).astype(BF)
    total = jnp.zeros((16, 128), F32)
    for y in range(4):
        total = total + mm(sely[y], neg[:, y * 128:y * 128 + 128])
    block[...] = total.astype(BF)
    halo_start(targets, block, slots, send3, recv3)
    halo_wait(targets, block, slots, send3, recv3)
    out[...] = slots[...]
    out[4] = block[...]


def backward_kernel(slots, sel, t4, w2, t5, s, r, slope1, slope2, a2,
                    adj, terms, sg, rm, gl):
    fill_shifts(sel, slots, sg)
    for z in range(8):
        grad = mm(t4[...], sg[(z + 1) * 48:(z + 1) * 48 + 144, :]) * slope2[z]
        for j in range(3):
            moved = shift(grad, j).astype(BF)
            for y in range(8):
                rm[z, y * 96 + j * 32:y * 96 + j * 32 + 32, :] = moved[y * 32:y * 32 + 32]
    for y in range(0, 6, 2):
        res = []
        for z in range(8):
            rhs = jnp.concatenate(
                [rm[z, y * 96:y * 96 + 288, :], rm[z, y * 96 + 96:y * 96 + 384, :]], axis=1)
            res.append(mm(w2[...], rhs))
        for z in range(6):
            grad = res[z][0:32] + res[z + 1][32:64] + res[z + 2][64:96]
            for q in range(2):
                yy = y + q
                at = slice(yy * 32, yy * 32 + 32)
                gl[z, at, :] = (grad[:, q * 128:q * 128 + 128] * slope1[z, at, :]).astype(BF)
    res = [mm(t5[...], gl[z]) for z in range(6)]
    for z in range(4):
        total = jnp.zeros((8, 128), F32)
        for j in range(3):
            part = res[z][j * 24:j * 24 + 8] + res[z + 1][j * 24 + 8:j * 24 + 16] \
                + res[z + 2][j * 24 + 16:j * 24 + 24]
            total = total + shift(part, j)
        adj[z] = total
    mid = jnp.zeros((288, 96), F32)
    none = jnp.zeros((32, 512), BF)
    own = [
        jnp.concatenate(
            [rm[z + 2, (y + 2) * 96 + 32:(y + 2) * 96 + 64, :] for y in range(4)], axis=1)
        for z in range(4)
    ]
    for t in range(6):
        lhs = jnp.concatenate(
            [r[t + 2, (y + 2) * 96:(y + 2) * 96 + 288, :] for y in range(4)], axis=1)
        rhs = jnp.concatenate(
            [own[t - j] if 0 <= t - j < 4 else none for j in range(3)], axis=0)
        mid = mid + mm_nt(lhs, rhs)
    terms[...] = jnp.zeros_like(terms)
    terms[0:288, 0:96] = mid
    first = jnp.zeros((144, 128), F32)
    for z in range(4):
        first = first + mm_nt(s[(z + 3) * 48:(z + 3) * 48 + 144, :], gl[z + 1, 32:160, :])
    third = jnp.zeros((144, 192), F32)
    blank = jnp.zeros((48, 128), BF)
    for t in range(6):
        lhs = jnp.concatenate(
            [sg[(4 + t - j) * 48:(5 + t - j) * 48, :] if 0 <= t - j < 4 else blank
             for j in range(3)], axis=0)
        third = third + mm_nt(lhs, a2[t])
    third = jnp.concatenate([third, jnp.zeros((144, 64), F32)], axis=1)
    row = lax.rem(lax.broadcasted_iota(jnp.int32, (144, 128), 0), 16)
    group = lax.broadcasted_iota(jnp.int32, (144, 128), 1) // 32
    for jy in range(3):
        pick = jnp.where(row == group + (3 + jy), first, 0.0).reshape(9, 16, 128).sum(axis=1)
        terms[288 + jy * 16:288 + jy * 16 + 16, :] = jnp.concatenate(
            [pick, jnp.zeros((7, 128), F32)], axis=0)
        own_row = (row >= 4) & (row < 8)
        pick = jnp.where(own_row & (row - 4 + jy == group), third[:, 0:128], 0.0) \
            + jnp.where(own_row & (row - 4 + jy == group + 4), third[:, 128:256], 0.0)
        pick = pick.reshape(9, 16, 128).sum(axis=1)
        terms[336 + jy * 16:336 + jy * 16 + 16, :] = jnp.concatenate(
            [pick, jnp.zeros((7, 128), F32)], axis=0)


def sum_kernel(depth, plane, terms, out, got, part, other, mine, ag, s1, r1, s2, r2, s3, r3):
    d, p = lax.axis_index("depth"), lax.axis_index("plane")
    bar = pltpu.get_barrier_semaphore()
    for i in range(1, plane):
        pl.semaphore_signal(bar, inc=1, device_id=(d, lax.rem(p + i, plane)), device_id_type=MESH)
    for i in range(1, depth):
        pl.semaphore_signal(bar, inc=1, device_id=(lax.rem(d + i, depth), p), device_id_type=MESH)
    pl.semaphore_wait(bar, plane + depth - 2)

    def first(i):
        to = lax.rem(p + i, plane)
        return pltpu.make_async_remote_copy(
            src_ref=terms.at[to], dst_ref=got.at[i], send_sem=s1.at[i], recv_sem=r1.at[i],
            device_id=(d, to), device_id_type=MESH)

    def second(i):
        return pltpu.make_async_remote_copy(
            src_ref=part, dst_ref=other.at[i], send_sem=s2.at[i], recv_sem=r2.at[i],
            device_id=(lax.rem(d + i, depth), p), device_id_type=MESH)

    def third(i):
        return pltpu.make_async_remote_copy(
            src_ref=mine, dst_ref=ag.at[p], send_sem=s3.at[i], recv_sem=r3.at[i],
            device_id=(d, lax.rem(p + i, plane)), device_id_type=MESH)

    for i in range(1, plane):
        first(i).start()
    total = terms[p].astype(F32)
    for i in range(1, plane):
        first(i).wait_recv()
        total = total + got[i].astype(F32)
    part[...] = total
    for i in range(1, depth):
        second(i).start()
    for i in range(1, depth):
        second(i).wait_recv()
    other[0] = total
    total = jnp.zeros_like(total)
    for k in range(depth):
        total = total + other[lax.rem(d - k + depth, depth)]
    mine[...] = total.astype(BF)
    for i in range(1, plane):
        third(i).start()
    for i in range(1, plane):
        third(i).wait_recv()
        first(i).wait_send()
        third(i).wait_send()
    for i in range(1, depth):
        second(i).wait_send()
    ag[p] = mine[...]
    out[...] = ag[...].astype(F32)


def tall(kernel, rows, off):
    where = np.zeros((3, rows, 16), np.float32)
    for jy in range(3):
        for y in range(rows):
            where[jy, y, y + off + jy - 1] = 1.0
    k = kernel.reshape(3, 3, 3, -1)
    full = jnp.einsum("zyxc,yab->aczxb", k, jnp.asarray(where, BF), preferred_element_type=F32)
    return full.reshape(rows * k.shape[3], 144).astype(BF)


def flat(kernel):
    where = np.zeros((3, 8, 6), np.float32)
    for jy in range(3):
        for y in range(4):
            where[jy, y + 4, y + jy] = 1.0
    k = kernel.reshape(3, 3, 3, -1)
    full = jnp.einsum("zyxc,yab->xzabc", k, jnp.asarray(where, BF), preferred_element_type=F32)
    return full.reshape(72, 6 * k.shape[3]).astype(BF)


def square(kernel):
    o, c = kernel.shape[1:]
    k = kernel.reshape(3, 3, 3, o, c)
    return k.transpose(0, 3, 1, 2, 4).reshape(3 * o, 9 * c)


def selectors():
    sel = np.zeros((192, 144), np.float32)
    for z in range(12):
        for y in range(12):
            sel[z * 16 + y, ((z // 4) * 3 + y // 4) * 16 + (z % 4) * 4 + y % 4] = 1.0
    selp = np.zeros((64, 96), np.float32)
    for y in range(4):
        for z in range(4):
            for k in range(2):
                selp[y * 16 + k * 8 + z, k * 48 + z * 8 + 4 + y] = 1.0
                selp[y * 16 + k * 8 + 4 + z, k * 48 + 32 + z * 4 + y] = 1.0
    sely = np.zeros((4, 16, 16), np.float32)
    for y in range(4):
        for z in range(4):
            sely[y, z * 4 + y, z] = 1.0
    return [jnp.asarray(x, BF) for x in (sel, selp, sely)]


def call(body, outs, scratch, args, cid=None):
    vm = pl.BlockSpec(memory_space=pltpu.VMEM)
    extra = {} if cid is None else dict(collective_id=cid, has_side_effects=True)
    return pl.pallas_call(
        body,
        out_shape=[jax.ShapeDtypeStruct(s, t) for s, t in outs],
        in_specs=[vm] * len(args),
        out_specs=[vm] * len(outs),
        scratch_shapes=scratch,
        compiler_params=pltpu.CompilerParams(vmem_limit_bytes=VMEM_LIMIT, **extra),
    )(*args)


def per_device(volume, cotangent, kernel_in, kernel_mid, kernel_out, measured, angle_ids, ray_bins):
    depth, plane = lax.axis_size("depth"), lax.axis_size("plane")
    nz, nh, width = volume.shape
    chan = kernel_in.shape[1]
    sem = pltpu.SemaphoreType.DMA
    sel, selp, sely = selectors()
    lanes = 8 * 512 // plane
    per = 512 // lanes
    bins = ray_bins.reshape(32, 128)
    t1 = tall(kernel_in, 10, 1)
    t4 = tall(kernel_out[::-1], 8, 2)
    t3 = flat(kernel_out)
    t5 = flat(kernel_in[::-1])
    w2f = square(kernel_mid)
    w2b = square(kernel_mid[::-1].transpose(0, 2, 1))
    chosen = jnp.take(measured, angle_ids, axis=1)
    chosen = chosen.reshape(4, 8, 2, per, lanes).transpose(1, 3, 2, 0, 4)
    chosen = jnp.pad(chosen, ((0, 0), (0, 0), (0, 0), (0, 4), (0, 0))).reshape(plane, 16, lanes)

    vol_slots = call(
        functools.partial(halo_kernel, depth, plane), [((9, 16, 128), BF)],
        [pltpu.VMEM((9, 16, 128), BF), sem((9,)), sem((9,))],
        [volume.reshape(16, 128)], 0)[0]
    s, r, slope1, slope2, a2, proj = call(
        functools.partial(forward_kernel, depth, plane, lanes),
        [((576, 128), BF), ((10, 960, 128), BF), ((6, 192, 128), F32), ((8, 256, 128), F32),
         ((6, 192, 128), BF), ((plane, 16, lanes), F32)],
        [], [vol_slots, sel, t1, w2f, t3, selp, cotangent.reshape(16, 128), bins])
    cot_rows = jnp.pad(cotangent.reshape(4, 512), ((0, 12), (0, 0)))
    gd, grad_slots = call(
        functools.partial(rays_kernel, depth, plane, lanes),
        [((16, 512), F32), ((9, 16, 128), BF)],
        [pltpu.VMEM((8192, 512), BF), pltpu.VMEM((plane, 16, lanes), F32),
         pltpu.VMEM((16, lanes), BF), pltpu.VMEM((plane, 16, lanes), BF),
         pltpu.VMEM((16, 128), BF), pltpu.VMEM((9, 16, 128), BF),
         sem((plane,)), sem((plane,)), sem((plane,)), sem((plane,)), sem((9,)), sem((9,))],
        [proj, chosen, bins, cot_rows, sely], 1)
    chunk = 16 * plane
    rows = -(-384 // chunk) * chunk
    adj, terms = call(
        backward_kernel, [((4, 8, 128), F32), ((rows, 128), F32)],
        [pltpu.VMEM((576, 128), BF), pltpu.VMEM((8, 768, 128), BF), pltpu.VMEM((6, 192, 128), BF)],
        [grad_slots, sel, t4, w2b, t5, s, r, slope1, slope2, a2])
    each = rows // plane
    summed = call(
        functools.partial(sum_kernel, depth, plane), [((plane, each, 128), F32)],
        [pltpu.VMEM((plane, each, 128), F32), pltpu.VMEM((each, 128), F32),
         pltpu.VMEM((depth, each, 128), F32), pltpu.VMEM((each, 128), BF),
         pltpu.VMEM((plane, each, 128), BF),
         sem((plane,)), sem((plane,)), sem((depth,)), sem((depth,)), sem((plane,)), sem((plane,))],
        [terms.reshape(plane, each, 128)], 2)[0].reshape(rows, 128)
    scale = float(nz * depth * nh * plane * width) ** -0.5
    grad_volume = gd[:4].reshape(4, 4, 128) + adj[:, 4:8, :]
    mid = summed[:288, :96].reshape(3, 3, chan, 3, chan).transpose(3, 0, 1, 4, 2)
    mid = mid.reshape(27, chan, chan)
    small = summed[288:384].reshape(2, 3, 16, 4, chan).sum(axis=3)[:, :, :9]
    small = small.reshape(2, 3, 3, 3, chan).transpose(0, 2, 1, 3, 4)
    first = small[0].reshape(27, chan)
    third = small[1][:, :, ::-1].reshape(27, chan)
    return (grad_volume, first * scale, mid * scale, third * scale)


def solution(mesh):
    placed = (
        P("depth", "plane", None),
        P("depth", "plane", None),
        P(),
        P(),
        P(),
        P("depth", None, None),
        P(),
        P(None, "plane", None),
    )
    return jax.shard_map(
        per_device,
        mesh=mesh,
        in_specs=placed,
        out_specs=(P("depth", "plane", None), P(), P(), P()),
        check_vma=False,
    )
```

profile of v0, /device:TPU:0, one launch (start us, length us, event | category | flops | bytes accessed | tf_op | source)
XLA Modules:
  0.0 80.1 jit_solution(15241144611655227539)
XLA Ops:
  0.7 8.0 %shard_map.174.slots = bf16[9,16,128]{2,1,0:T(8,128)(2,1)} custom-call(bf16[16,128]{1,0:T(8,128)(2,1)} %bitcast.89), custom_call_target="tpu_custom_call" | custom-call | tf_op jit(solution)/shard_map/pallas_call | solution.py:435
  8.7 0.7 reshape.100
  9.4 1.0 %fusion = bf16[10,32,3,3,16]{1,4,3,2,0:T(8,128)(2,1)S(1)} fusion(bf16[3,10,16,1,1]{2,0,4,3,1:T(4,128)(2,1)} %constant.48, bf16[3,3,3,32]{3,2,1,0:T(4,128)(2,1)S(1)} %reshape.100), kind=kOutput, calls=%fused_computation.3 | convolution fusion | flops 322560 | bytes 94848 | tf_op jit(solution)/shard_map/zyxc,yab->aczxb/dot_general | solution.py:394
  10.6 0.3 convert_element_type.34
  10.9 0.8 copy.66.t1
  11.9 0.8 %reshape.102.w2 = bf16[96,288]{1,0:T(8,128)(2,1)} reshape(bf16[3,32,3,3,32]{4,3,2,1,0:T(4,128)(2,1)S(1)} %bitcast.74) | data formatting | bytes 110592 | tf_op jit(solution)/shard_map/reshape | solution.py:411
  13.0 0.8 convert_element_type.37.t3
  13.7 8.8 %shard_map.175 = (bf16[576,128]{1,0:T(8,128)(2,1)}, bf16[10,960,128]{2,1,0:T(8,128)(2,1)}, f32[6,192,128]{2,1,0:T(8,128)}, f32[8,256,128]{2,1,0:T(8,128)}, bf16[...) custom-call(bf16[9,16,128]{2,1,0:T(8,128)(2,1)} %shard_map.174.slots, bf16[192,144]{1,0:T(8,128)(2,1)} %constant.35.clone.sel, ...), custom_call_target="tpu_custom_call" | custom-call | tf_op jit(solution)/shard_map/pallas_call | solution.py:435
  22.6 0.7 gather_fusion
  23.5 0.7 pad_bitcast_fusion.chosen
  24.3 0.6 pad.9.cot
  24.9 21.2 %shard_map.176 = (f32[16,512]{1,0:T(8,128)}, bf16[9,16,128]{2,1,0:T(8,128)(2,1)}) custom-call(f32[8,16,512]{2,1,0:T(8,128)} %get-tuple-element.14.proj, f32[8,16,512]{2,1,0:T(8,128)} %pad_bitcast_fusion.chosen, s32[32,128]{1,0:T(8,128)} %bitcast.85, f32[16,512]{1,0:T(8,128)} %pad.9.cot, bf16[4,16,16]{2,1,0:T(8,128)(2,1)} %constant.37.clone.sely), custom_call_target="tpu_custom_call" | custom-call | tf_op jit(solution)/shard_map/pallas_call | solution.py:435
  46.1 0.7 slice.22
  47.4 0.8 copy.73.t4
  48.4 0.8 %reshape.111.w2 = bf16[96,288]{1,0:T(8,128)(2,1)} reshape(bf16[3,32,3,3,32]{4,3,2,1,0:T(4,128)(2,1)S(1)} %bitcast.73) | data formatting | bytes 110592 | tf_op jit(solution)/shard_map/reshape | solution.py:411
  49.5 0.8 convert_element_type.43.t5
  50.3 5.8 %shard_map.177 = (f32[4,8,128]{2,1,0:T(8,128)}, f32[384,128]{1,0:T(8,128)}) custom-call(bf16[9,16,128]{2,1,0:T(8,128)(2,1)} %get-tuple-element.16.slots, bf16[192,144]{1,0:T(8,128)(2,1)} %constant.35.clone.sel, bf16[256,144]{1,0:T(8,128)(2,1)} %copy.73.t4, bf16[96,288]{1,0:T(8,128)(2,1)} %reshape.111.w2, bf16[72,192]{1,0:T(8,128)(2,1)} %convert_element_type.43.t5, ...), custom_call_target="tpu_custom_call" | custom-call | tf_op jit(solution)/shard_map/pallas_call | solution.py:435
  56.1 1.3 %slice_add_fusion = f32[4,4,128]{2,1,0:T(4,128)} fusion(f32[4,4,128]{2,1,0:T(4,128)S(1)} %reshape.108, f32[4,8,128]{2,1,0:T(8,128)} %get-tuple-element.22), kind=kLoop, calls=%fused_computation.26 | loop fusion | flops 2048 | bytes 24576 | tf_op jit(solution)/shard_map/add | solution.py:497
  57.4 18.1 %shard_map.178 = f32[8,48,128]{2,1,0:T(8,128)} custom-call(f32[8,48,128]{2,1,0:T(8,128)} %bitcast.80), custom_call_target="tpu_custom_call" | custom-call | tf_op jit(solution)/shard_map/pallas_call | solution.py:435
  75.5 0.8 %slice.24 = f32[2,48,128]{2,1,0:T(8,128)S(1)} slice(f32[8,48,128]{2,1,0:T(8,128)} %shard_map.178), slice={[6:8], [0:48], [0:128]} | slice | bytes 98304 | tf_op jit(solution)/shard_map/slice | solution.py:500
  76.7 0.6 mul.28
  77.3 0.9 %slice_multiply_fusion = f32[288,96]{1,0:T(8,128)S(1)} fusion(f32[384,128]{1,0:T(8,128)} %bitcast.77), kind=kLoop, calls=%fused_computation.11 | loop fusion | flops 27648 | bytes 221184 | tf_op jit(solution)/shard_map/mul | solution.py:504
  78.5 1.0 %copy.76 = f32[3,3,3,32,32]{4,3,2,1,0:T(8,128)} copy(f32[3,3,3,32,32]{3,0,4,2,1:T(4,128)S(1)} %bitcast.72) | data formatting | bytes 221184 | tf_op jit(solution)/shard_map/mul | solution.py:504
  79.5 0.6 mul.35
  (48 shorter events, 2.5 us)
Async XLA Ops:
  0.6 22.0 %copy-start = (f32[4,32,1024]{2,1,0:T(8,128)S(1)}, f32[4,32,1024]{2,1,0:T(8,128)}, u32[]{:S(2)}) copy-start(f32[4,32,1024]{2,1,0:T(8,128)} %param.20) | copy-start | bytes 1572868
  0.6 12.1 %copy-start.5 = (bf16[3,8,6,1,1]{1,0,4,3,2:T(4,128)(2,1)S(1)}, bf16[3,8,6,1,1]{1,0,4,3,2:T(4,128)(2,1)}, u32[]{:S(2)}) copy-start(bf16[3,8,6,1,1]{1,0,4,3,2:T(4,128)(2,1)} %constant.49) | copy-start | bytes 868
  0.7 11.1 %copy-start.1 = (bf16[27,32,32]{2,1,0:T(8,128)(2,1)S(1)}, bf16[27,32,32]{2,1,0:T(8,128)(2,1)}, u32[]{:S(2)}) copy-start(bf16[27,32,32]{2,1,0:T(8,128)(2,1)} %param.18) | copy-start | bytes 165892
  0.7 12.0 %copy-start.3 = (bf16[27,32]{1,0:T(8,128)(2,1)S(1)}, bf16[27,32]{1,0:T(8,128)(2,1)}, u32[]{:S(2)}) copy-start(bf16[27,32]{1,0:T(8,128)(2,1)} %param.19) | copy-start | bytes 5188
  0.7 21.9 %copy-start.7 = (s32[8]{0:T(128)S(1)}, s32[8]{0:T(128)}, u32[]{:S(2)}) copy-start(s32[8]{0:T(128)} %param.21) | copy-start | bytes 100
  10.6 13.7 %copy-start.2 = (f32[4,4,128]{2,1,0:T(4,128)S(1)}, f32[4,4,128]{2,1,0:T(4,128)}, u32[]{:S(2)}) copy-start(f32[4,4,128]{2,1,0:T(4,128)} %param.16) | copy-start | bytes 24580
  10.9 35.9 %copy-start.6 = (bf16[3,8,16,1,1]{2,0,4,3,1:T(4,128)(2,1)S(1)}, bf16[3,8,16,1,1]{2,0,4,3,1:T(4,128)(2,1)}, u32[]{:S(2)}) copy-start(bf16[3,8,16,1,1]{2,0,4,3,1:T(4,128)(2,1)} %constant.50) | copy-start | bytes 2308
  22.6 26.6 %copy-start.4 = (bf16[27,32]{1,0:T(8,128)(2,1)S(1)}, bf16[27,32]{1,0:T(8,128)(2,1)}, u32[]{:S(2)}) copy-start(bf16[27,32]{1,0:T(8,128)(2,1)} %param.17) | copy-start | bytes 5188
where the time goes:
time: 80.6 us; the launch traced here: 80.1 us
  Pallas kernels  61.9 us (77%)
  local copies, waits for them, and re-layouts  13 us (16%)
  other arithmetic  2.51 us (3%)
  matrix products  1.74 us (2%)
  between operations  0.94 us (1%)
    pallas_call x5, Pallas kernels, call(): pl.pallas_call(body, out_shape=[jax.ShapeDtypeStruct(s, t) for s, t in ou...  61.9 us
    mul x6, local copies, waits for them, and re-layouts, per_device(): return (grad_volume, first * scale, mid * scale, third * scale)  2.45 us
    convert_element_type x6, local copies, waits for them, and re-layouts, tall(): return full.reshape(rows * k.shape[3], 144).astype(BF)  2.27 us
    reshape x2, local copies, waits for them, and re-layouts, square(): return k.transpose(0, 3, 1, 2, 4).reshape(3 * o, 9 * c)  1.63 us

commit v1 on v0

--- a/solution.py
+++ b/solution.py
@@ -72,7 +72,99 @@
             halo_copy(-dz, -dy, who, mine, slots, send, recv).wait_recv()
 
 
-def halo_kernel(depth, plane, block, out, slots, send, recv):
+def iota(shape, dim):
+    return lax.broadcasted_iota(jnp.int32, shape, dim)
+
+
+def ones_where(mask):
+    return jnp.where(mask, 1.0, 0.0).astype(BF)
+
+
+def tall(k, rows, off, flip):
+    chan = k.shape[1]
+    pick = ones_where(lax.rem(iota((rows * chan, chan), 0), chan) == iota((rows * chan, chan), 1))
+    wide = mm_nt(pick, k).astype(BF)
+    shape = (rows * chan, 144)
+    y_in = lax.rem(iota(shape, 1), 16)
+    y = iota(shape, 0) // chan
+    col = iota((27, 144), 1)
+    total = jnp.zeros(shape, F32)
+    for jy in range(3):
+        src = (col // 48) * 9 + jy * 3 + lax.rem(col // 16, 3)
+        if flip:
+            src = 26 - src
+        part = mm(wide, ones_where(iota((27, 144), 0) == src))
+        total = total + jnp.where(y_in == y + (off + jy - 1), part, 0.0)
+    return total.astype(BF)
+
+
+def flat(k, flip):
+    chan = k.shape[1]
+    shape = (72, 6 * chan)
+    y = lax.rem(iota(shape, 0), 8)
+    y_in = iota(shape, 1) // chan
+    spread = ones_where(lax.rem(iota((chan, 6 * chan), 1), chan) == iota((chan, 6 * chan), 0))
+    row = iota((72, 27), 0)
+    total = jnp.zeros(shape, F32)
+    for jy in range(3):
+        src = lax.rem(row // 8, 3) * 9 + jy * 3 + row // 24
+        if flip:
+            src = 26 - src
+        part = mm(mm(ones_where(iota((72, 27), 1) == src), k).astype(BF), spread)
+        total = total + jnp.where((y >= 4) & (y_in == y - 4 + jy), part, 0.0)
+    return total.astype(BF)
+
+
+def square(k):
+    chan = k.shape[1]
+    total = jnp.zeros((3 * chan, 9 * chan), F32)
+    for q in range(9):
+        rows = jnp.concatenate([k[j * 9 + q] for j in range(3)], axis=0)
+        place = ones_where(iota((chan, 9 * chan), 1) == iota((chan, 9 * chan), 0) + q * chan)
+        total = total + mm(rows, place)
+    return total.astype(BF)
+
+
+def square_back(k):
+    chan = k.shape[1]
+    eye = ones_where(iota((chan, chan), 0) == iota((chan, chan), 1))
+    return jnp.concatenate(
+        [mm_nt(eye, jnp.concatenate([k[26 - j * 9 - q] for q in range(9)], axis=0))
+         for j in range(3)], axis=0).astype(BF)
+
+
+def fill_shifts(sel, slots, dst):
+    flat = slots[...].reshape(9 * 16, 128)
+    wide = mm(sel[...], flat)
+    for z in range(12):
+        rows = wide[z * 16:(z + 1) * 16]
+        for j in range(3):
+            dst[z * 48 + j * 16:z * 48 + (j + 1) * 16, :] = shift(rows, j).astype(BF)
+    return wide
+
+
+def keep_rows(shape, z, margin, depth, plane):
+    d, p = lax.axis_index("depth"), lax.axis_index("plane")
+    gz = d * 4 + z - margin
+    row = lax.broadcasted_iota(jnp.int32, shape, 0)
+    low = (margin - p * 4) * 32
+    high = (plane * 4 + margin - p * 4) * 32
+    high = jnp.where((gz >= 0) & (gz < depth * 4), high, -1)
+    return (row >= low) & (row < high)
+
+
+def build_onehot(bins, a, c, size):
+    parts = []
+    for y in range(4):
+        row = bins[pl.ds(a * 4 + y, 1), :]
+        at = lax.broadcasted_iota(jnp.int32, (size, 128), 0) + c * size
+        parts.append(jnp.where(at == row, 1.0, 0.0).astype(BF))
+    return jnp.concatenate(parts, axis=1)
+
+
+def forward_kernel(depth, plane, lanes, block, sel, k1, k2, k3, selp, cot, bins,
+                   s_out, r_out, slope1, slope2, a2, proj,
+                   slots, t1, w2, t3, send, recv):
     targets = halo_targets(depth, plane)
     slots[...] = jnp.zeros_like(slots)
     bar = pltpu.get_barrier_semaphore()
@@ -84,42 +176,11 @@
         count = count + there.astype(jnp.int32)
     pl.semaphore_wait(bar, count)
     halo_start(targets, block, slots, send, recv)
+    t1[...] = tall(k1[...], 10, 1, False)
+    w2[...] = square(k2)
+    t3[...] = flat(k3[...], False)
     halo_wait(targets, block, slots, send, recv)
-    out[...] = slots[...]
-    out[4] = block[...]
-
-
-def fill_shifts(sel, slots, dst):
-    flat = slots[...].reshape(9 * 16, 128)
-    wide = mm(sel[...], flat)
-    for z in range(12):
-        rows = wide[z * 16:(z + 1) * 16]
-        for j in range(3):
-            dst[z * 48 + j * 16:z * 48 + (j + 1) * 16, :] = shift(rows, j).astype(BF)
-    return wide
-
-
-def keep_rows(shape, z, margin, depth, plane):
-    d, p = lax.axis_index("depth"), lax.axis_index("plane")
-    gz = d * 4 + z - margin
-    row = lax.broadcasted_iota(jnp.int32, shape, 0)
-    low = (margin - p * 4) * 32
-    high = (plane * 4 + margin - p * 4) * 32
-    high = jnp.where((gz >= 0) & (gz < depth * 4), high, -1)
-    return (row >= low) & (row < high)
-
-
-def build_onehot(bins, a, c, size):
-    parts = []
-    for y in range(4):
-        row = bins[pl.ds(a * 4 + y, 1), :]
-        at = lax.broadcasted_iota(jnp.int32, (size, 128), 0) + c * size
-        parts.append(jnp.where(at == row, 1.0, 0.0).astype(BF))
-    return jnp.concatenate(parts, axis=1)
-
-
-def forward_kernel(depth, plane, lanes, slots, sel, t1, w2, t3, selp, cot, bins,
-                   s_out, r_out, slope1, slope2, a2, proj):
+    slots[4] = block[...]
     wide = fill_shifts(sel, slots, s_out)
     for z in range(10):
         pre = mm(t1[...], s_out[z * 48:z * 48 + 144, :])
@@ -182,7 +243,8 @@
     lax.fori_loop(0, 8, view, 0)
 
 
-def rays_kernel(depth, plane, lanes, proj, chosen, bins, cot, sely, gd_out, out,
+def rays_kernel(depth, plane, lanes, proj, chosen, bins, cot, sely, k1, k2, k3,
+                gd_out, out, t4, w2, t5,
                 onehot, got, mine, ag, block, slots, send1, recv1, send2, recv2, send3, recv3):
     d, p = lax.axis_index("depth"), lax.axis_index("plane")
     targets = halo_targets(depth, plane)
@@ -221,6 +283,9 @@
         return carry
 
     lax.fori_loop(0, 32, fill, 0)
+    t4[...] = tall(k3[...], 8, 2, True)
+    w2[...] = square_back(k2)
+    t5[...] = flat(k1[...], True)
     total = proj[p]
     for i in range(1, plane):
         first(i).wait_recv()
@@ -263,8 +328,15 @@
     out[4] = block[...]
 
 
-def backward_kernel(slots, sel, t4, w2, t5, s, r, slope1, slope2, a2,
-                    adj, terms, sg, rm, gl):
+def backward_kernel(depth, plane, scale, slots, sel, t4, w2, t5, s, r, slope1, slope2, a2,
+                    adj, out1, out2, out3, terms, sg, rm, gl,
+                    got, part, other, mine, ag, s1, r1, s2, r2, s3, r3):
+    d, p = lax.axis_index("depth"), lax.axis_index("plane")
+    bar = pltpu.get_barrier_semaphore()
+    for i in range(1, plane):
+        pl.semaphore_signal(bar, inc=1, device_id=(d, lax.rem(p + i, plane)), device_id_type=MESH)
+    for i in range(1, depth):
+        pl.semaphore_signal(bar, inc=1, device_id=(lax.rem(d + i, depth), p), device_id_type=MESH)
     fill_shifts(sel, slots, sg)
     for z in range(8):
         grad = mm(t4[...], sg[(z + 1) * 48:(z + 1) * 48 + 144, :]) * slope2[z]
@@ -288,9 +360,9 @@
     for z in range(4):
         total = jnp.zeros((8, 128), F32)
         for j in range(3):
-            part = res[z][j * 24:j * 24 + 8] + res[z + 1][j * 24 + 8:j * 24 + 16] \
+            piece = res[z][j * 24:j * 24 + 8] + res[z + 1][j * 24 + 8:j * 24 + 16] \
                 + res[z + 2][j * 24 + 16:j * 24 + 24]
-            total = total + shift(part, j)
+            total = total + shift(piece, j)
         adj[z] = total
     mid = jnp.zeros((288, 96), F32)
     none = jnp.zeros((32, 512), BF)
@@ -330,21 +402,16 @@
         pick = pick.reshape(9, 16, 128).sum(axis=1)
         terms[336 + jy * 16:336 + jy * 16 + 16, :] = jnp.concatenate(
             [pick, jnp.zeros((7, 128), F32)], axis=0)
-
-
-def sum_kernel(depth, plane, terms, out, got, part, other, mine, ag, s1, r1, s2, r2, s3, r3):
-    d, p = lax.axis_index("depth"), lax.axis_index("plane")
-    bar = pltpu.get_barrier_semaphore()
-    for i in range(1, plane):
-        pl.semaphore_signal(bar, inc=1, device_id=(d, lax.rem(p + i, plane)), device_id_type=MESH)
-    for i in range(1, depth):
-        pl.semaphore_signal(bar, inc=1, device_id=(lax.rem(d + i, depth), p), device_id_type=MESH)
     pl.semaphore_wait(bar, plane + depth - 2)
+    each = terms.shape[0] // plane
+
+    def rows_of(q):
+        return terms.at[pl.ds(pl.multiple_of(q * each, each), each)]
 
     def first(i):
         to = lax.rem(p + i, plane)
         return pltpu.make_async_remote_copy(
-            src_ref=terms.at[to], dst_ref=got.at[i], send_sem=s1.at[i], recv_sem=r1.at[i],
+            src_ref=rows_of(to), dst_ref=got.at[i], send_sem=s1.at[i], recv_sem=r1.at[i],
             device_id=(d, to), device_id_type=MESH)
 
     def second(i):
@@ -359,10 +426,10 @@
 
     for i in range(1, plane):
         first(i).start()
-    total = terms[p].astype(F32)
+    total = rows_of(p)[...]
     for i in range(1, plane):
         first(i).wait_recv()
-        total = total + got[i].astype(F32)
+        total = total + got[i]
     part[...] = total
     for i in range(1, depth):
         second(i).start()
@@ -382,33 +449,20 @@
     for i in range(1, depth):
         second(i).wait_send()
     ag[p] = mine[...]
-    out[...] = ag[...].astype(F32)
-
-
-def tall(kernel, rows, off):
-    where = np.zeros((3, rows, 16), np.float32)
-    for jy in range(3):
-        for y in range(rows):
-            where[jy, y, y + off + jy - 1] = 1.0
-    k = kernel.reshape(3, 3, 3, -1)
-    full = jnp.einsum("zyxc,yab->aczxb", k, jnp.asarray(where, BF), preferred_element_type=F32)
-    return full.reshape(rows * k.shape[3], 144).astype(BF)
-
-
-def flat(kernel):
-    where = np.zeros((3, 8, 6), np.float32)
-    for jy in range(3):
-        for y in range(4):
-            where[jy, y + 4, y + jy] = 1.0
-    k = kernel.reshape(3, 3, 3, -1)
-    full = jnp.einsum("zyxc,yab->xzabc", k, jnp.asarray(where, BF), preferred_element_type=F32)
-    return full.reshape(72, 6 * k.shape[3]).astype(BF)
-
-
-def square(kernel):
-    o, c = kernel.shape[1:]
-    k = kernel.reshape(3, 3, 3, o, c)
-    return k.transpose(0, 3, 1, 2, 4).reshape(3 * o, 9 * c)
+    summed = ag[...].reshape(plane * each, 128)
+    chan = out2.shape[1]
+    for j in range(3):
+        pick = ones_where(iota((chan, 128), 1) == iota((chan, 128), 0) + j * chan)
+        for q in range(9):
+            out2[j * 9 + q] = mm_nt(pick, summed[q * chan:(q + 1) * chan]) * scale
+    fold = ones_where(lax.rem(iota((128, chan), 0), chan) == iota((128, chan), 1))
+    k = iota((32, 48), 0)
+    for at, flip, out in ((288, False, out1), (336, True, out3)):
+        jx = lax.rem(k, 3)
+        jx = 2 - jx if flip else jx
+        order = ones_where(iota((32, 48), 1) == lax.rem(k // 3, 3) * 16 + (k // 9) * 3 + jx)
+        moved = mm(order, summed[at:at + 48]).astype(BF)
+        out[...] = mm(moved, fold)[0:27] * scale
 
 
 def selectors():
@@ -451,57 +505,44 @@
     lanes = 8 * 512 // plane
     per = 512 // lanes
     bins = ray_bins.reshape(32, 128)
-    t1 = tall(kernel_in, 10, 1)
-    t4 = tall(kernel_out[::-1], 8, 2)
-    t3 = flat(kernel_out)
-    t5 = flat(kernel_in[::-1])
-    w2f = square(kernel_mid)
-    w2b = square(kernel_mid[::-1].transpose(0, 2, 1))
     chosen = jnp.take(measured, angle_ids, axis=1)
     chosen = chosen.reshape(4, 8, 2, per, lanes).transpose(1, 3, 2, 0, 4)
     chosen = jnp.pad(chosen, ((0, 0), (0, 0), (0, 0), (0, 4), (0, 0))).reshape(plane, 16, lanes)
 
-    vol_slots = call(
-        functools.partial(halo_kernel, depth, plane), [((9, 16, 128), BF)],
-        [pltpu.VMEM((9, 16, 128), BF), sem((9,)), sem((9,))],
-        [volume.reshape(16, 128)], 0)[0]
     s, r, slope1, slope2, a2, proj = call(
         functools.partial(forward_kernel, depth, plane, lanes),
         [((576, 128), BF), ((10, 960, 128), BF), ((6, 192, 128), F32), ((8, 256, 128), F32),
          ((6, 192, 128), BF), ((plane, 16, lanes), F32)],
-        [], [vol_slots, sel, t1, w2f, t3, selp, cotangent.reshape(16, 128), bins])
+        [pltpu.VMEM((9, 16, 128), BF), pltpu.VMEM((10 * chan, 144), BF),
+         pltpu.VMEM((3 * chan, 9 * chan), BF), pltpu.VMEM((72, 6 * chan), BF), sem((9,)), sem((9,))],
+        [volume.reshape(16, 128), sel, kernel_in, kernel_mid, kernel_out, selp,
+         cotangent.reshape(16, 128), bins], 0)
     cot_rows = jnp.pad(cotangent.reshape(4, 512), ((0, 12), (0, 0)))
-    gd, grad_slots = call(
+    gd, grad_slots, t4, w2b, t5 = call(
         functools.partial(rays_kernel, depth, plane, lanes),
-        [((16, 512), F32), ((9, 16, 128), BF)],
+        [((16, 512), F32), ((9, 16, 128), BF), ((8 * chan, 144), BF),
+         ((3 * chan, 9 * chan), BF), ((72, 6 * chan), BF)],
         [pltpu.VMEM((8192, 512), BF), pltpu.VMEM((plane, 16, lanes), F32),
          pltpu.VMEM((16, lanes), BF), pltpu.VMEM((plane, 16, lanes), BF),
          pltpu.VMEM((16, 128), BF), pltpu.VMEM((9, 16, 128), BF),
          sem((plane,)), sem((plane,)), sem((plane,)), sem((plane,)), sem((9,)), sem((9,))],
-        [proj, chosen, bins, cot_rows, sely], 1)
+        [proj, chosen, bins, cot_rows, sely, kernel_in, kernel_mid, kernel_out], 1)
     chunk = 16 * plane
     rows = -(-384 // chunk) * chunk
-    adj, terms = call(
-        backward_kernel, [((4, 8, 128), F32), ((rows, 128), F32)],
-        [pltpu.VMEM((576, 128), BF), pltpu.VMEM((8, 768, 128), BF), pltpu.VMEM((6, 192, 128), BF)],
-        [grad_slots, sel, t4, w2b, t5, s, r, slope1, slope2, a2])
     each = rows // plane
-    summed = call(
-        functools.partial(sum_kernel, depth, plane), [((plane, each, 128), F32)],
-        [pltpu.VMEM((plane, each, 128), F32), pltpu.VMEM((each, 128), F32),
+    scale = float(nz * depth * nh * plane * width) ** -0.5
+    adj, first, mid, third = call(
+        functools.partial(backward_kernel, depth, plane, scale),
+        [((4, 8, 128), F32), ((27, chan), F32), ((27, chan, chan), F32), ((27, chan), F32)],
+        [pltpu.VMEM((rows, 128), F32),
+         pltpu.VMEM((576, 128), BF), pltpu.VMEM((8, 768, 128), BF), pltpu.VMEM((6, 192, 128), BF),
+         pltpu.VMEM((plane, each, 128), F32), pltpu.VMEM((each, 128), F32),
          pltpu.VMEM((depth, each, 128), F32), pltpu.VMEM((each, 128), BF),
          pltpu.VMEM((plane, each, 128), BF),
          sem((plane,)), sem((plane,)), sem((depth,)), sem((depth,)), sem((plane,)), sem((plane,))],
-        [terms.reshape(plane, each, 128)], 2)[0].reshape(rows, 128)
-    scale = float(nz * depth * nh * plane * width) ** -0.5
+        [grad_slots, sel, t4, w2b, t5, s, r, slope1, slope2, a2], 2)
     grad_volume = gd[:4].reshape(4, 4, 128) + adj[:, 4:8, :]
-    mid = summed[:288, :96].reshape(3, 3, chan, 3, chan).transpose(3, 0, 1, 4, 2)
-    mid = mid.reshape(27, chan, chan)
-    small = summed[288:384].reshape(2, 3, 16, 4, chan).sum(axis=3)[:, :, :9]
-    small = small.reshape(2, 3, 3, 3, chan).transpose(0, 2, 1, 3, 4)
-    first = small[0].reshape(27, chan)
-    third = small[1][:, :, ::-1].reshape(27, chan)
-    return (grad_volume, first * scale, mid * scale, third * scale)
+    return (grad_volume, first, mid, third)
 
 
 def solution(mesh):

time: 80.6 us -> 69.8 us (0.87)
  local copies, waits for them, and re-layouts: 13 us -> 7.97 us
  Pallas kernels: 61.9 us -> 57.6 us
  matrix products: 1.74 us -> 0 us
    unnamed x18 -> x6, local copies, waits for them, and re-layouts: 0.06 us -> 5.16 us
    pallas_call x5 -> x3, Pallas kernels: 61.9 us -> 57.6 us  [call(): pl.pallas_call(body, out_shape=[jax.ShapeDtypeStruct(s, t) for s, t in ou...]
    convert_element_type x10 -> x0, local copies, waits for them, and re-layouts: 3.85 us -> none  [the longest x6 2.27 us: tall(): return full.reshape(rows * k.shape[3], 144).astype(BF)]
    reshape x9 -> x0, local copies, waits for them, and re-layouts: 2.88 us -> none  [the longest x2 1.63 us: square(): return k.transpose(0, 3, 1, 2, 4).reshape(3 * o, 9 * c)]
    mul x6 -> x0, local copies, waits for them, and re-layouts: 2.45 us -> none  [per_device(): return (grad_volume, first * scale, mid * scale, third * scale)]
    dot_general x4 -> x0, matrix products: 1.74 us -> none  [the longest x2 1.3 us: tall(): jnp.einsum('zyxc,yab->aczxb', k, jnp.asarray(where, BF), preferred_elemen...]
    mul x2 -> x0, other arithmetic: 0.93 us -> none  [per_device(): return (grad_volume, first * scale, mid * scale, third * scale)]
    slice x2 -> x0, local copies, waits for them, and re-layouts: 0.82 us -> none  [per_device(): small = summed[288:384].reshape(2, 3, 16, 4, chan).sum(axis=3)[:, :, :9]]
where the time goes in v1:
time: 69.8 us; the launch traced here: 69.1 us
  Pallas kernels  57.6 us (83%)
  local copies, waits for them, and re-layouts  7.97 us (11%)
  other arithmetic  2.81 us (4%)
    pallas_call x3, Pallas kernels, call(): pl.pallas_call(body, out_shape=[jax.ShapeDtypeStruct(s, t) for s, t in ou...  57.6 us
    unnamed x6, local copies, waits for them, and re-layouts  5.16 us

profile of v1, /device:TPU:0, one launch (start us, length us, event | category | flops | bytes accessed | tf_op | source)
XLA Modules:
  0.0 69.1 jit_solution(15345131349579011727)
XLA Ops:
  0.6 0.0 copy-start
  0.6 0.7 %compare_and_fusion = pred[8]{0:T(512)(128)(4,1)S(1)} fusion(s32[8]{0:T(128)} %param.17), kind=kLoop, calls=%fused_computation.8 | loop fusion | flops 48 | bytes 40 | tf_op jit(solution)/shard_map/jit(_take)/and | solution.py:508
  1.4 0.7 compare_select_fusion
  2.0 0.7 %copy.22 = f32[1,4,4,128]{3,1,2,0:T(4,128)S(1)} copy(f32[1,4,4,128]{3,2,1,0:T(4,128)} %bitcast.17) | data formatting | bytes 16384
  2.7 0.6 pad.9.cot
  3.3 0.0 copy-done
  3.3 0.7 %gather_fusion = f32[8,4,1024]{2,0,1:T(8,128)S(1)} fusion(f32[4,32,1024]{2,1,0:T(8,128)S(1)} %copy-done, s32[1024]{0:T(1024)S(1)} %pad_clamp_fusion), kind=kCustom, calls=%fused_computation | custom fusion | bytes 262176 | tf_op jit(solution)/shard_map/jit(_take)/gather | solution.py:508
  4.1 0.1 fusion
  4.2 0.7 %pad_bitcast_fusion.chosen = f32[8,16,512]{2,1,0:T(8,128)} fusion(f32[8,1,2,4,512]{4,3,2,0,1:T(4,128)S(1)} %fusion), kind=kLoop, calls=%fused_computation.1 | loop fusion | bytes 393216 | tf_op jit(solution)/shard_map/reshape | solution.py:510
  4.9 15.4 %shard_map.138 = (bf16[576,128]{1,0:T(8,128)(2,1)}, bf16[10,960,128]{2,1,0:T(8,128)(2,1)}, f32[6,192,128]{2,1,0:T(8,128)}, f32[8,256,128]{2,1,0:T(8,128)}, bf16[...) custom-call(bf16[16,128]{1,0:T(8,128)(2,1)} %bitcast.20, bf16[192,144]{1,0:T(8,128)(2,1)} %constant.25.clone.sel, ...), custom_call_target="tpu_custom_call" | custom-call | tf_op jit(solution)/shard_map/pallas_call | solution.py:489
  20.3 21.4 %shard_map.139 = (f32[16,512]{1,0:T(8,128)}, bf16[9,16,128]{2,1,0:T(8,128)(2,1)}, bf16[256,144]{1,0:T(8,128)(2,1)}, bf16[96,288]{1,0:T(8,128)(2,1)}, bf16[72,192]{1,0:T(8,128)(2,1)}) custom-call(f32[8,16,512]{2,1,0:T(8,128)} %get-tuple-element.19.proj, f32[8,16,512]{2,1,0:T(8,128)} %pad_bitcast_fusion.chosen, s32[32,128]{1,0:T(8,128)} %bitcast.16, ...), custom_call_target="tpu_custom_call" | custom-call | tf_op jit(solution)/shard_map/pallas_call | solution.py:489
  41.8 20.8 %shard_map.140 = (f32[4,8,128]{2,1,0:T(8,128)}, f32[27,32]{1,0:T(8,128)}, f32[27,32,32]{2,1,0:T(8,128)}, f32[27,32]{1,0:T(8,128)}) custom-call(bf16[9,16,128]{2,1,0:T(8,128)(2,1)} %get-tuple-element.21.slots, bf16[192,144]{1,0:T(8,128)(2,1)} %constant.25.clone.sel, bf16[256,144]{1,0:T(8,128)(2,1)} %get-tuple-element.22.t4, ...), custom_call_target="tpu_custom_call" | custom-call | tf_op jit(solution)/shard_map/pallas_call | solution.py:489
  62.6 0.7 %slice.6 = f32[4,512]{1,0:T(4,128)S(1)} slice(f32[16,512]{1,0:T(8,128)} %get-tuple-element.20), slice={[0:4], [0:512]} | slice | bytes 16384 | tf_op jit(solution)/shard_map/slice | solution.py:544
  63.3 1.3 %slice_add_fusion = f32[4,4,128]{2,1,0:T(4,128)} fusion(f32[4,4,128]{2,1,0:T(4,128)S(1)} %reshape.47, f32[4,8,128]{2,1,0:T(8,128)} %get-tuple-element.30), kind=kLoop, calls=%fused_computation.5 | loop fusion | flops 2048 | bytes 24576 | tf_op jit(solution)/shard_map/add | solution.py:544
  64.6 1.3 %copy.26 = f32[27,32]{1,0:T(8,128)} copy(f32[27,32]{1,0:T(8,128)} %get-tuple-element.39) | data formatting | bytes 6912
  65.9 1.8 %copy.27 = f32[27,32,32]{2,1,0:T(8,128)} copy(f32[27,32,32]{2,1,0:T(8,128)} %get-tuple-element.40) | data formatting | bytes 221184
  67.7 1.3 %copy.28 = f32[27,32]{1,0:T(8,128)} copy(f32[27,32]{1,0:T(8,128)} %get-tuple-element.41) | data formatting | bytes 6912
  (2 shorter events, 0.0 us)
Async XLA Ops:
  0.6 2.7 %copy-start = (f32[4,32,1024]{2,1,0:T(8,128)S(1)}, f32[4,32,1024]{2,1,0:T(8,128)}, u32[]{:S(2)}) copy-start(f32[4,32,1024]{2,1,0:T(8,128)} %param.16) | copy-start | bytes 1572868

commit v2 on v1

--- a/solution.py
+++ b/solution.py
@@ -164,7 +164,7 @@
 
 def forward_kernel(depth, plane, lanes, block, sel, k1, k2, k3, selp, cot, bins,
                    s_out, r_out, slope1, slope2, a2, proj,
-                   slots, t1, w2, t3, send, recv):
+                   slots, t1, w2, t3, onehot, send, recv):
     targets = halo_targets(depth, plane)
     slots[...] = jnp.zeros_like(slots)
     bar = pltpu.get_barrier_semaphore()
@@ -179,6 +179,13 @@
     t1[...] = tall(k1[...], 10, 1, False)
     w2[...] = square(k2)
     t3[...] = flat(k3[...], False)
+
+    def fill(k, carry):
+        onehot[pl.ds(pl.multiple_of(k * 256, 256), 256), :] = build_onehot(
+            bins, k // 4, lax.rem(k, 4), 256)
+        return carry
+
+    lax.fori_loop(0, 32, fill, 0)
     halo_wait(targets, block, slots, send, recv)
     slots[4] = block[...]
     wide = fill_shifts(sel, slots, s_out)
@@ -232,7 +239,8 @@
         for half in range(2):
             row = []
             for c in range(2):
-                got = mm_nt(lhs, build_onehot(bins, a, half * 2 + c, 256))
+                at = pl.multiple_of(a * 1024 + (half * 2 + c) * 256, 256)
+                got = mm_nt(lhs, onehot[pl.ds(at, 256), :])
                 row.append(got[0:8] + got[8:16])
             halves.append(jnp.concatenate(row, axis=1))
         full = jnp.concatenate(halves, axis=0)
@@ -315,8 +323,9 @@
     back = low + up
     back = back + pltpu.roll(back, 12, 0)
     row = lax.broadcasted_iota(jnp.int32, (16, 512), 0)
-    gd = jnp.where(row < 4, cot[...] - back * (0.25 / 8), 0.0)
-    gd_out[...] = gd
+    cot16 = jnp.concatenate([cot[...], jnp.zeros((12, 512), F32)], axis=0)
+    gd = jnp.where(row < 4, cot16 - back * (0.25 / 8), 0.0)
+    gd_out[...] = gd[0:4]
     neg = (-gd).astype(BF)
     total = jnp.zeros((16, 128), F32)
     for y in range(4):
@@ -328,7 +337,7 @@
     out[4] = block[...]
 
 
-def backward_kernel(depth, plane, scale, slots, sel, t4, w2, t5, s, r, slope1, slope2, a2,
+def backward_kernel(depth, plane, slots, sel, t4, w2, t5, s, r, slope1, slope2, a2,
                     adj, out1, out2, out3, terms, sg, rm, gl,
                     got, part, other, mine, ag, s1, r1, s2, r2, s3, r3):
     d, p = lax.axis_index("depth"), lax.axis_index("plane")
@@ -356,14 +365,6 @@
                 yy = y + q
                 at = slice(yy * 32, yy * 32 + 32)
                 gl[z, at, :] = (grad[:, q * 128:q * 128 + 128] * slope1[z, at, :]).astype(BF)
-    res = [mm(t5[...], gl[z]) for z in range(6)]
-    for z in range(4):
-        total = jnp.zeros((8, 128), F32)
-        for j in range(3):
-            piece = res[z][j * 24:j * 24 + 8] + res[z + 1][j * 24 + 8:j * 24 + 16] \
-                + res[z + 2][j * 24 + 16:j * 24 + 24]
-            total = total + shift(piece, j)
-        adj[z] = total
     mid = jnp.zeros((288, 96), F32)
     none = jnp.zeros((32, 512), BF)
     own = [
@@ -426,6 +427,14 @@
 
     for i in range(1, plane):
         first(i).start()
+    res = [mm(t5[...], gl[z]) for z in range(6)]
+    for z in range(4):
+        total = jnp.zeros((8, 128), F32)
+        for j in range(3):
+            piece = res[z][j * 24:j * 24 + 8] + res[z + 1][j * 24 + 8:j * 24 + 16] \
+                + res[z + 2][j * 24 + 16:j * 24 + 24]
+            total = total + shift(piece, j)
+        adj[z] = total
     total = rows_of(p)[...]
     for i in range(1, plane):
         first(i).wait_recv()
@@ -454,7 +463,7 @@
     for j in range(3):
         pick = ones_where(iota((chan, 128), 1) == iota((chan, 128), 0) + j * chan)
         for q in range(9):
-            out2[j * 9 + q] = mm_nt(pick, summed[q * chan:(q + 1) * chan]) * scale
+            out2[j * 9 + q] = mm_nt(pick, summed[q * chan:(q + 1) * chan])
     fold = ones_where(lax.rem(iota((128, chan), 0), chan) == iota((128, chan), 1))
     k = iota((32, 48), 0)
     for at, flip, out in ((288, False, out1), (336, True, out3)):
@@ -462,7 +471,7 @@
         jx = 2 - jx if flip else jx
         order = ones_where(iota((32, 48), 1) == lax.rem(k // 3, 3) * 16 + (k // 9) * 3 + jx)
         moved = mm(order, summed[at:at + 48]).astype(BF)
-        out[...] = mm(moved, fold)[0:27] * scale
+        out[...] = mm(moved, fold)[0:27]
 
 
 def selectors():
@@ -514,13 +523,14 @@
         [((576, 128), BF), ((10, 960, 128), BF), ((6, 192, 128), F32), ((8, 256, 128), F32),
          ((6, 192, 128), BF), ((plane, 16, lanes), F32)],
         [pltpu.VMEM((9, 16, 128), BF), pltpu.VMEM((10 * chan, 144), BF),
-         pltpu.VMEM((3 * chan, 9 * chan), BF), pltpu.VMEM((72, 6 * chan), BF), sem((9,)), sem((9,))],
+         pltpu.VMEM((3 * chan, 9 * chan), BF), pltpu.VMEM((72, 6 * chan), BF),
+         pltpu.VMEM((8192, 512), BF), sem((9,)), sem((9,))],
         [volume.reshape(16, 128), sel, kernel_in, kernel_mid, kernel_out, selp,
          cotangent.reshape(16, 128), bins], 0)
-    cot_rows = jnp.pad(cotangent.reshape(4, 512), ((0, 12), (0, 0)))
+    cot_rows = cotangent.reshape(4, 512)
     gd, grad_slots, t4, w2b, t5 = call(
         functools.partial(rays_kernel, depth, plane, lanes),
-        [((16, 512), F32), ((9, 16, 128), BF), ((8 * chan, 144), BF),
+        [((4, 512), F32), ((9, 16, 128), BF), ((8 * chan, 144), BF),
          ((3 * chan, 9 * chan), BF), ((72, 6 * chan), BF)],
         [pltpu.VMEM((8192, 512), BF), pltpu.VMEM((plane, 16, lanes), F32),
          pltpu.VMEM((16, lanes), BF), pltpu.VMEM((plane, 16, lanes), BF),
@@ -532,7 +542,7 @@
     each = rows // plane
     scale = float(nz * depth * nh * plane * width) ** -0.5
     adj, first, mid, third = call(
-        functools.partial(backward_kernel, depth, plane, scale),
+        functools.partial(backward_kernel, depth, plane),
         [((4, 8, 128), F32), ((27, chan), F32), ((27, chan, chan), F32), ((27, chan), F32)],
         [pltpu.VMEM((rows, 128), F32),
          pltpu.VMEM((576, 128), BF), pltpu.VMEM((8, 768, 128), BF), pltpu.VMEM((6, 192, 128), BF),
@@ -541,8 +551,8 @@
          pltpu.VMEM((plane, each, 128), BF),
          sem((plane,)), sem((plane,)), sem((depth,)), sem((depth,)), sem((plane,)), sem((plane,))],
         [grad_slots, sel, t4, w2b, t5, s, r, slope1, slope2, a2], 2)
-    grad_volume = gd[:4].reshape(4, 4, 128) + adj[:, 4:8, :]
-    return (grad_volume, first, mid, third)
+    grad_volume = gd.reshape(4, 4, 128) + adj[:, 4:8, :]
+    return (grad_volume, first * scale, mid * scale, third * scale)
 
 
 def solution(mesh):

time: 69.8 us -> 67 us (0.960)
  local copies, waits for them, and re-layouts: 7.97 us -> 2.79 us
  other arithmetic: 2.81 us -> 5.97 us
    unnamed x6 -> x5, local copies, waits for them, and re-layouts: 5.16 us -> 1.31 us
    mul x0 -> x2, other arithmetic: none -> 3.16 us  [per_device(): return (grad_volume, first * scale, mid * scale, third * scale)]
    slice x1 -> x0, local copies, waits for them, and re-layouts: 0.72 us -> none  [per_device(): grad_volume = gd[:4].reshape(4, 4, 128) + adj[:, 4:8, :]]
where the time goes in v2:
time: 67 us; the launch traced here: 66.4 us
  Pallas kernels  57 us (85%)
  other arithmetic  5.97 us (9%)
  local copies, waits for them, and re-layouts  2.79 us (4%)
  between operations  0.7 us (1%)
    pallas_call x3, Pallas kernels, call(): pl.pallas_call(body, out_shape=[jax.ShapeDtypeStruct(s, t) for s, t in ou...  57 us
    mul x2, other arithmetic, per_device(): return (grad_volume, first * scale, mid * scale, third * scale)  3.16 us

profile of v2, /device:TPU:0, one launch (start us, length us, event | category | flops | bytes accessed | tf_op | source)
XLA Modules:
  0.0 66.4 jit_solution(13493266380854113407)
XLA Ops:
  0.6 0.0 copy-start
  0.6 0.7 %compare_and_fusion = pred[8]{0:T(512)(128)(4,1)S(1)} fusion(s32[8]{0:T(128)} %param.17), kind=kLoop, calls=%fused_computation.11 | loop fusion | flops 48 | bytes 40 | tf_op jit(solution)/shard_map/jit(_take)/and | solution.py:517
  1.4 0.7 compare_select_fusion
  2.0 1.3 %copy.22 = f32[1,4,4,128]{3,1,2,0:T(4,128)} copy(f32[1,4,4,128]{3,2,1,0:T(4,128)} %bitcast.18) | data formatting | bytes 16384
  3.3 0.0 copy-done
  3.3 0.7 %gather_fusion = f32[8,4,1024]{2,0,1:T(8,128)S(1)} fusion(f32[4,32,1024]{2,1,0:T(8,128)S(1)} %copy-done, s32[1024]{0:T(1024)S(1)} %pad_clamp_fusion), kind=kCustom, calls=%fused_computation | custom fusion | bytes 262176 | tf_op jit(solution)/shard_map/jit(_take)/gather | solution.py:517
  4.1 0.1 fusion
  4.2 0.7 %pad_bitcast_fusion.chosen = f32[8,16,512]{2,1,0:T(8,128)} fusion(f32[8,1,2,4,512]{4,3,2,0,1:T(4,128)S(1)} %fusion), kind=kLoop, calls=%fused_computation.1 | loop fusion | bytes 393216 | tf_op jit(solution)/shard_map/reshape | solution.py:519
  4.9 15.4 %shard_map.138 = (bf16[576,128]{1,0:T(8,128)(2,1)}, bf16[10,960,128]{2,1,0:T(8,128)(2,1)}, f32[6,192,128]{2,1,0:T(8,128)}, f32[8,256,128]{2,1,0:T(8,128)}, bf16[...) custom-call(bf16[16,128]{1,0:T(8,128)(2,1)} %bitcast.20, bf16[192,144]{1,0:T(8,128)(2,1)} %constant.28.clone.sel, ...), custom_call_target="tpu_custom_call" | custom-call | tf_op jit(solution)/shard_map/pallas_call | solution.py:498
  20.4 21.4 %shard_map.139 = (f32[4,512]{1,0:T(4,128)}, bf16[9,16,128]{2,1,0:T(8,128)(2,1)}, bf16[256,144]{1,0:T(8,128)(2,1)}, bf16[96,288]{1,0:T(8,128)(2,1)}, bf16[72,192]{1,0:T(8,128)(2,1)}) custom-call(f32[8,16,512]{2,1,0:T(8,128)} %get-tuple-element.19.proj, f32[8,16,512]{2,1,0:T(8,128)} %pad_bitcast_fusion.chosen, s32[32,128]{1,0:T(8,128)} %bitcast.16, ...), custom_call_target="tpu_custom_call" | custom-call | tf_op jit(solution)/shard_map/pallas_call | solution.py:498
  41.8 0.0 copy-start.1
  41.8 20.1 %shard_map.140 = (f32[4,8,128]{2,1,0:T(8,128)}, f32[27,32]{1,0:T(8,128)}, f32[27,32,32]{2,1,0:T(8,128)}, f32[27,32]{1,0:T(8,128)}) custom-call(bf16[9,16,128]{2,1,0:T(8,128)(2,1)} %get-tuple-element.21.slots, bf16[192,144]{1,0:T(8,128)(2,1)} %constant.28.clone.sel, bf16[256,144]{1,0:T(8,128)(2,1)} %get-tuple-element.22.t4, ...), custom_call_target="tpu_custom_call" | custom-call | tf_op jit(solution)/shard_map/pallas_call | solution.py:498
  61.9 0.0 copy-done.1
  61.9 1.3 %slice_add_fusion = f32[4,4,128]{2,1,0:T(4,128)} fusion(f32[4,4,128]{2,1,0:T(4,128)S(1)} %reshape.47, f32[4,8,128]{2,1,0:T(8,128)} %get-tuple-element.30), kind=kLoop, calls=%fused_computation.8 | loop fusion | flops 2048 | bytes 24576 | tf_op jit(solution)/shard_map/add | solution.py:554
  63.3 1.3 %broadcast_multiply_fusion.1 = (f32[27,32]{1,0:T(8,128)}, f32[27,32]{1,0:T(8,128)}) fusion(f32[27,32]{1,0:T(8,128)} %get-tuple-element.33, f32[27,32]{1,0:T(8,128)} %get-tuple-element.31), kind=kLoop, calls=%fused_computation.6 | loop fusion | flops 1728 | bytes 13824 | tf_op jit(solution)/shard_map/mul | solution.py:555
  64.6 1.8 %broadcast_multiply_fusion = f32[27,32,32]{2,1,0:T(8,128)} fusion(f32[27,32,32]{2,1,0:T(8,128)} %get-tuple-element.32), kind=kLoop, calls=%fused_computation.2 | loop fusion | flops 27648 | bytes 221184 | tf_op jit(solution)/shard_map/mul | solution.py:555
  (2 shorter events, 0.0 us)
Async XLA Ops:
  0.6 2.7 %copy-start = (f32[4,32,1024]{2,1,0:T(8,128)S(1)}, f32[4,32,1024]{2,1,0:T(8,128)}, u32[]{:S(2)}) copy-start(f32[4,32,1024]{2,1,0:T(8,128)} %param.16) | copy-start | bytes 1572868
  41.8 20.1 %copy-start.1 = (f32[4,512]{1,0:T(4,128)S(1)}, f32[4,512]{1,0:T(4,128)}, u32[]{:S(2)}) copy-start(f32[4,512]{1,0:T(4,128)} %get-tuple-element.20) | copy-start | bytes 24580
